TPU v7x, 512 devices: a whole 4x8x8 slice. The times are simulated.
512 devices in a mesh: row: 16 (over z, core), col: 32 (over x, y).
Axes of the slice: x: 4, y: 8, z: 8, core: 2. Of those that a mesh axis runs over, the one named last changes fastest.
Arguments:
- front: float32 [12288, 12288], P('row', 'col'), as said below
- structure: int32 [3, 96], replicated, may hold values from 0 to 1, as said below
- factor_front: float32 [3, 12288, 512], P(None, 'row', 'col'), may hold values from -0.0546875 to 0.0546875
- factor_border: float32 [2, 512, 512], replicated, may hold values from -0.6 to 0.6
- pivot_inverse: float32 [3, 512, 512], P(None, 'row')
Outputs:
- inverse_front: float32 [3, 512, 12288], P(None, 'row', 'col')
- inverse_parent: float32 [2, 512, 512], P(None, 'row')
- inverse_diagonal: float32 [3, 512, 512], P(None, 'row')
Inputs may be any that keep to these rules, and one draw needn't show every extreme that they name: front is exactly symmetric. structure[k, b] = 1 where front block b (rows b * 128 to (b + 1) * 128 - 1) lies in supernode k's structure; every 1 in row k is also a 1 in row k - 1; blocks b < 24 are 1 in every row.
All inputs are finite; a program needn't handle non-finite values.
Results may differ from a plain program's by a relative error of at most 0.0001.
Values sent between devices are 32-bit elements; how exact they have to be, the bound alone decides.
A program may use at most 64 MiB of HBM per device.

v0:
```python
import jax
import jax.numpy as jnp
from jax import lax
from jax.sharding import Mesh
from jax.sharding import PartitionSpec as P

BLK = 128
ROW = ("row_0", "row_1")
HIGH = lax.Precision.HIGHEST


def broadcast_by_axis(x, axes, root):
    x = jnp.where(lax.axis_index(axes) == root, x, jnp.zeros_like(x))
    for axis in axes:
        x = lax.psum(x, axis)
    return x


def split_up(x, dim, length):
    dims = x.shape
    pieces = x.reshape(*dims[:dim], length, dims[dim] // length, *dims[dim + 1 :])
    return jnp.moveaxis(pieces, dim, 0)


def sent_and_summed(x, axis, dim):
    length = lax.axis_size(axis)
    pieces = lax.all_to_all(split_up(x, dim, length), axis, 0, 0, tiled=True)
    return jnp.sum(pieces, axis=0)


def padded_to(lines, length):
    spare = -lines.shape[0] % length
    if not spare:
        return lines
    return jnp.concatenate([lines, jnp.zeros((spare, *lines.shape[1:]), lines.dtype)])


def in_order(pieces, dim):
    pieces = jnp.moveaxis(pieces, 0, dim)
    dims = pieces.shape
    return pieces.reshape(*dims[:dim], dims[dim] * dims[dim + 1], *dims[dim + 2 :])


def from_everyone(x, axis):
    copies = jnp.broadcast_to(x, (lax.axis_size(axis), *x.shape))
    return lax.all_to_all(copies, axis, split_axis=0, concat_axis=0, tiled=True)


def collect(x, axis, dim):
    return in_order(from_everyone(x, axis), dim)


def total_of(x, axes):
    lines = x.reshape(-1, x.shape[-1])
    own = sent_and_summed(padded_to(lines, lax.axis_size(axes)), axes, 0)
    whole = collect(own, axes, 0)
    return whole[: len(lines)].reshape(x.shape)


def matmul(former, latter):
    return jnp.dot(former, latter, precision=HIGH, preferred_element_type=jnp.float32)


def contract_first(former, latter):
    return lax.dot_general(
        former, latter, (((0,), (0,)), ((), ())), precision=HIGH, preferred_element_type=jnp.float32
    )


def block_flags(structure_row, first_row, rows_count):
    position = first_row + jnp.arange(rows_count, dtype=jnp.int32)
    owners = position // BLK
    numbers = jnp.arange(structure_row.shape[0], dtype=jnp.int32)
    matches = (owners[:, None] == numbers[None, :]).astype(jnp.float32)
    return jnp.dot(matches, structure_row.astype(jnp.float32), precision=HIGH)


def body(front, structure, factor_front, factor_border, pivot_inverse):
    row_index = lax.axis_index(ROW)
    col_index = lax.axis_index("col")
    rows_here = front.shape[0]
    cols_here = front.shape[1]
    width_here = pivot_inverse.shape[1]
    supers = structure.shape[0]
    row_first = row_index * rows_here
    col_first = col_index * cols_here
    fetched = lax.all_gather(factor_front, "col", axis=2, tiled=True)
    fronts = []
    parents = []
    diagonals = []
    previous = None
    diag_prev = None
    for section in range(supers):
        gathered = fetched[section]
        row_flags = block_flags(structure[section], row_first, rows_here)
        factor_rows = gathered * row_flags[:, None]
        own_half = lax.dynamic_slice_in_dim(factor_rows, col_index % 2 * cols_here, cols_here, 0)
        factor_cols = broadcast_by_axis(own_half, ROW, col_index // 2)
        partial_value = contract_first(factor_rows, front)
        if section > 0:
            border = factor_border[section - 1]
            border_rows = lax.dynamic_slice_in_dim(border, row_index * width_here, width_here, 0)
            partial_value = partial_value + contract_first(border_rows, previous)
            parent_part = total_of(matmul(previous, factor_cols), "col")
            parent_rows = parent_part + matmul(diag_prev, border)
            parent_all = lax.all_gather(parent_rows, ROW, axis=0, tiled=True)
            parents.append(-parent_rows)
        image_rows = sent_and_summed(partial_value, ROW, 0)
        col_flags = block_flags(structure[section], col_first, cols_here)
        current = -(image_rows * col_flags[None, :])
        gram_rows = total_of(matmul(image_rows, factor_cols), "col")
        diag_now = pivot_inverse[section] + gram_rows
        if section > 0:
            parent_slice = lax.dynamic_slice_in_dim(
                parent_all, row_index * width_here, width_here, 1
            )
            diag_now = diag_now + contract_first(parent_slice, border)
        fronts.append(current)
        diagonals.append(diag_now)
        previous = current
        diag_prev = diag_now
    return (jnp.stack(fronts), jnp.stack(parents), jnp.stack(diagonals))


def solution(mesh):
    torus = Mesh(mesh.devices.reshape(8, 2, mesh.shape["col"]), ("row_0", "row_1", "col"))
    return jax.shard_map(
        body,
        mesh=torus,
        in_specs=(P(ROW, "col"), P(), P(None, ROW, "col"), P(), P(None, ROW, None)),
        out_specs=(P(None, ROW, "col"), P(None, ROW, None), P(None, ROW, None)),
        check_vma=False,
    )
```

profile of v0, /device:TPU:1, one launch (start us, length us, event | category | flops | bytes accessed | tf_op | source)
XLA Modules:
  0.0 465.4 jit_solution(13938320989205049159)
XLA Ops:
  11.3 91.5 %all-gather.4.cloned.1.call-done = f32[3,768,512]{1,2,0:T(8,128)} async-done(((f32[3,768,16]{1,2,0:T(8,128)}), f32[3,768,512]{1,2,0:T(8,128)}) %all-gather.4.cloned.1.call-update) | async-done | bytes 4718608 | tf_op jit(solution)/shard_map/all_gather | solution.py:87
  108.1 87.4 %all-reduce.5.cloned.1.call-done = (f32[384,512]{0,1:T(8,128)}, f32[384,512]{0,1:T(8,128)}, f32[384,512]{0,1:T(8,128)}) async-done(((f32[384,512]{0,1:T(8,128)}, f32[384,512]{0,1:T(8,128)}, f32[384,512]{0,1:T(8,128)}), (f32[384,512]{0,1:T(8,128)}, f32[384,512]{0,1:T(8,128)}, f32[384,512]{0,1:T(8,128)})) %all-reduce.5.cloned.1.call-update) | async-done | bytes 2359312 | tf_op jit(solution)/shard_map/psum | solution.py:15
  199.1 8.3 %all-to-all-start = ((f32[16,32,384]{2,1,0:T(8,128)}), f32[16,32,384]{2,1,0:T(8,128)}, u32[]{:S(2)}, u32[]{:S(2)}) async-start(f32[16,32,384]{2,1,0:T(8,128)} %fusion.3), calls=%async_computation | async-start | bytes 1572864 | tf_op jit(solution)/shard_map/all_to_all | solution.py:27
  207.8 22.4 %all-to-all-done = f32[16,32,384]{2,1,0:T(8,128)} async-done(((f32[16,32,384]{2,1,0:T(8,128)}), f32[16,32,384]{2,1,0:T(8,128)}, u32[]{:S(2)}, u32[]{:S(2)}) %all-to-all-start) | async-done | bytes 786464 | tf_op jit(solution)/shard_map/all_to_all | solution.py:27
  231.4 8.4 %all-reduce.7.cloned.1.call-done = (f32[384,512]{0,1:T(8,128)}, f32[384,512]{0,1:T(8,128)}, f32[384,512]{0,1:T(8,128)}) async-done(((f32[384,512]{0,1:T(8,128)}, f32[384,512]{0,1:T(8,128)}, f32[384,512]{0,1:T(8,128)}), (f32[384,512]{0,1:T(8,128)}, f32[384,512]{0,1:T(8,128)}, f32[384,512]{0,1:T(8,128)})) %all-reduce.7.cloned.1.call-update) | async-done | bytes 2359312 | tf_op jit(solution)/shard_map/psum | solution.py:15
  242.5 8.3 %all-to-all-start.5 = ((f32[32,1,512]{2,1,0:T(1,128)}), f32[32,1,512]{2,1,0:T(1,128)S(1)}, u32[]{:S(2)}, u32[]{:S(2)}) async-start(f32[32,1,512]{2,1,0:T(1,128)} %copy.9), calls=%async_computation.5 | async-start | bytes 131072 | tf_op jit(solution)/shard_map/all_to_all | solution.py:27
  253.4 6.2 %all-to-all-done.5 = f32[32,1,512]{2,1,0:T(1,128)S(1)} async-done(((f32[32,1,512]{2,1,0:T(1,128)}), f32[32,1,512]{2,1,0:T(1,128)S(1)}, u32[]{:S(2)}, u32[]{:S(2)}) %all-to-all-start.5) | async-done | bytes 65568 | tf_op jit(solution)/shard_map/all_to_all | solution.py:27
  265.1 7.3 %all-to-all-done.3 = f32[32,1,512]{2,1,0:T(1,128)S(1)} async-done(((f32[32,1,512]{2,1,0:T(1,128)}), f32[32,1,512]{2,1,0:T(1,128)S(1)}, u32[]{:S(2)}, u32[]{:S(2)}) %all-to-all-start.3) | async-done | bytes 65568 | tf_op jit(solution)/shard_map/all_to_all | solution.py:27
  279.5 6.2 %all-to-all-done.6 = f32[32,1,512]{2,1,0:T(1,128)S(1)} async-done(((f32[32,1,512]{2,1,0:T(1,128)}), f32[32,1,512]{2,1,0:T(1,128)S(1)}, u32[]{:S(2)}, u32[]{:S(2)}) %all-to-all-start.6) | async-done | bytes 65568 | tf_op jit(solution)/shard_map/all_to_all | solution.py:46
  290.3 5.1 %convolution_add_fusion.1 = f32[512,384]{1,0:T(8,128)} fusion(f32[512,384]{1,0:T(8,128)} %fusion.21, f32[768,512]{0,1:T(8,128)} %copy-done.3, f32[768,384]{1,0:T(8,128)S(1)} %copy-done), kind=kOutput, calls=%fused_computation.7 | convolution fusion | flops 1812135936 | bytes 4325376 | tf_op jit(solution)/shard_map/dot_general | solution.py:65
  299.1 12.6 %all-to-all-start.1 = ((f32[16,32,384]{2,1,0:T(8,128)}), f32[16,32,384]{2,1,0:T(8,128)}, u32[]{:S(2)}, u32[]{:S(2)}) async-start(f32[16,32,384]{2,1,0:T(8,128)} %bitcast.123), calls=%async_computation.1 | async-start | bytes 1572864 | tf_op jit(solution)/shard_map/all_to_all | solution.py:27
  315.4 19.6 %all-to-all-done.1 = f32[16,32,384]{2,1,0:T(8,128)} async-done(((f32[16,32,384]{2,1,0:T(8,128)}), f32[16,32,384]{2,1,0:T(8,128)}, u32[]{:S(2)}, u32[]{:S(2)}) %all-to-all-start.1) | async-done | bytes 786464 | tf_op jit(solution)/shard_map/all_to_all | solution.py:27
  338.9 4.1 all-to-all-start.7
  345.7 6.2 %all-to-all-done.7 = f32[32,1,512]{2,1,0:T(1,128)S(1)} async-done(((f32[32,1,512]{2,1,0:T(1,128)}), f32[32,1,512]{2,1,0:T(1,128)S(1)}, u32[]{:S(2)}, u32[]{:S(2)}) %all-to-all-start.7) | async-done | bytes 65568 | tf_op jit(solution)/shard_map/all_to_all | solution.py:27
  357.3 8.5 %all-to-all-done.9 = f32[32,1,512]{2,1,0:T(1,128)S(1)} async-done(((f32[32,1,512]{2,1,0:T(1,128)}), f32[32,1,512]{2,1,0:T(1,128)S(1)}, u32[]{:S(2)}, u32[]{:S(2)}) %all-to-all-start.9) | async-done | bytes 65568 | tf_op jit(solution)/shard_map/all_to_all | solution.py:27
  373.8 5.4 %all-to-all-done.8 = f32[32,1,512]{2,1,0:T(1,128)S(1)} async-done(((f32[32,1,512]{2,1,0:T(1,128)}), f32[32,1,512]{2,1,0:T(1,128)S(1)}, u32[]{:S(2)}, u32[]{:S(2)}) %all-to-all-start.8) | async-done | bytes 65568 | tf_op jit(solution)/shard_map/all_to_all | solution.py:46
  379.9 4.6 all-to-all-start.10
  384.4 5.1 %convolution_add_fusion = f32[512,384]{1,0:T(8,128)} fusion(f32[512,384]{1,0:T(8,128)} %fusion.19, f32[768,512]{0,1:T(8,128)} %copy-done.2, f32[768,384]{1,0:T(8,128)S(1)} %copy-done), kind=kOutput, calls=%fused_computation.6 | convolution fusion | flops 1812135936 | bytes 4325376 | tf_op jit(solution)/shard_map/dot_general | solution.py:65
  393.4 7.4 %all-to-all-start.2 = ((f32[16,32,384]{2,1,0:T(8,128)}), f32[16,32,384]{2,1,0:T(8,128)}, u32[]{:S(2)}, u32[]{:S(2)}) async-start(f32[16,32,384]{2,1,0:T(8,128)} %bitcast.122), calls=%async_computation.2 | async-start | bytes 1572864 | tf_op jit(solution)/shard_map/all_to_all | solution.py:27
  406.8 17.4 %all-to-all-done.2 = f32[16,32,384]{2,1,0:T(8,128)} async-done(((f32[16,32,384]{2,1,0:T(8,128)}), f32[16,32,384]{2,1,0:T(8,128)}, u32[]{:S(2)}, u32[]{:S(2)}) %all-to-all-start.2) | async-done | bytes 786464 | tf_op jit(solution)/shard_map/all_to_all | solution.py:27
  428.0 4.6 all-to-all-start.11
  434.1 7.3 %all-to-all-done.11 = f32[32,1,512]{2,1,0:T(1,128)} async-done(((f32[32,1,512]{2,1,0:T(1,128)}), f32[32,1,512]{2,1,0:T(1,128)}, u32[]{:S(2)}, u32[]{:S(2)}) %all-to-all-start.11) | async-done | bytes 65568 | tf_op jit(solution)/shard_map/all_to_all | solution.py:27
  442.9 4.5 all-to-all-start.12
  449.0 7.4 %all-to-all-done.12 = f32[32,1,512]{2,1,0:T(1,128)} async-done(((f32[32,1,512]{2,1,0:T(1,128)}), f32[32,1,512]{2,1,0:T(1,128)}, u32[]{:S(2)}, u32[]{:S(2)}) %all-to-all-start.12) | async-done | bytes 65568 | tf_op jit(solution)/shard_map/all_to_all | solution.py:46
  (94 shorter events, 85.2 us)
Async XLA Ops:
  7.2 188.4 %copy-start = (f32[768,384]{1,0:T(8,128)S(1)}, f32[768,384]{1,0:T(8,128)}, u32[]{:S(2)}) copy-start(f32[768,384]{1,0:T(8,128)} %param.5) | copy-start | bytes 3538948
  7.2 95.6 %all-gather.4.cloned.1.call-start = ((), (), s32[]{:S(2)}) async-start(), calls=%async_computation.13 | async-start | bytes 4866048 | tf_op jit(solution)/shard_map/all_gather | solution.py:87
  7.9 187.6 %all-reduce.5.cloned.1.call-start = ((), (), s32[]{:S(2)}) async-start(), calls=%async_computation.16 | async-start | bytes 4718592 | tf_op jit(solution)/shard_map/psum | solution.py:15
  108.0 131.8 %all-reduce.7.cloned.1.call-start = ((), (), s32[]{:S(2)}) async-start(), calls=%async_computation.17 | async-start | bytes 4718592 | tf_op jit(solution)/shard_map/psum | solution.py:15
  199.1 31.1 %all-to-all-start = ((f32[16,32,384]{2,1,0:T(8,128)}), f32[16,32,384]{2,1,0:T(8,128)}, u32[]{:S(2)}, u32[]{:S(2)}) async-start(f32[16,32,384]{2,1,0:T(8,128)} %fusion.3), calls=%async_computation | async-start | bytes 1572864 | tf_op jit(solution)/shard_map/all_to_all | solution.py:27
  207.8 55.7 %copy-start.1 = (f32[2,512,512]{2,1,0:T(8,128)S(1)}, f32[2,512,512]{2,1,0:T(8,128)}, u32[]{:S(2)}) copy-start(f32[2,512,512]{2,1,0:T(8,128)} %param.8) | copy-start | bytes 6291460
  242.5 17.1 %all-to-all-start.5 = ((f32[32,1,512]{2,1,0:T(1,128)}), f32[32,1,512]{2,1,0:T(1,128)S(1)}, u32[]{:S(2)}, u32[]{:S(2)}) async-start(f32[32,1,512]{2,1,0:T(1,128)} %copy.9), calls=%async_computation.5 | async-start | bytes 131072 | tf_op jit(solution)/shard_map/all_to_all | solution.py:27
  259.6 12.7 %all-to-all-start.3 = ((f32[32,1,512]{2,1,0:T(1,128)}), f32[32,1,512]{2,1,0:T(1,128)S(1)}, u32[]{:S(2)}, u32[]{:S(2)}) async-start(f32[32,1,512]{2,1,0:T(1,128)} %copy.8), calls=%async_computation.3 | async-start | bytes 131072 | tf_op jit(solution)/shard_map/all_to_all | solution.py:27
  273.0 12.7 %all-to-all-start.6 = ((f32[32,1,512]{2,1,0:T(1,128)}), f32[32,1,512]{2,1,0:T(1,128)S(1)}, u32[]{:S(2)}, u32[]{:S(2)}) async-start(f32[32,1,512]{2,1,0:T(1,128)} %broadcast_in_dim.11), calls=%async_computation.6 | async-start | bytes 131072 | tf_op jit(solution)/shard_map/all_to_all | solution.py:46
  286.4 12.7 %all-to-all-start.4 = ((f32[32,1,512]{2,1,0:T(1,128)}), f32[32,1,512]{2,1,0:T(1,128)S(1)}, u32[]{:S(2)}, u32[]{:S(2)}) async-start(f32[32,1,512]{2,1,0:T(1,128)} %broadcast_in_dim.10), calls=%async_computation.4 | async-start | bytes 131072 | tf_op jit(solution)/shard_map/all_to_all | solution.py:46
  299.1 12.6 %copy-start.7 = (f32[32,1,512]{2,1,0:T(1,128)}, f32[32,1,512]{2,1,0:T(1,128)S(1)}, u32[]{:S(2)}) copy-start(f32[32,1,512]{2,1,0:T(1,128)S(1)} %all-to-all-done.4) | copy-start | bytes 196612
  299.1 35.9 %all-to-all-start.1 = ((f32[16,32,384]{2,1,0:T(8,128)}), f32[16,32,384]{2,1,0:T(8,128)}, u32[]{:S(2)}, u32[]{:S(2)}) async-start(f32[16,32,384]{2,1,0:T(8,128)} %bitcast.123), calls=%async_computation.1 | async-start | bytes 1572864 | tf_op jit(solution)/shard_map/all_to_all | solution.py:27
  311.7 89.1 %all-gather.6.cloned.1.call-start = ((), (), s32[]{:S(2)}) async-start(), calls=%async_computation.14 | async-start | bytes 1114112 | tf_op jit(solution)/shard_map/all_gather | solution.py:106
  338.9 13.0 %all-to-all-start.7 = ((f32[32,1,512]{2,1,0:T(1,128)}), f32[32,1,512]{2,1,0:T(1,128)S(1)}, u32[]{:S(2)}, u32[]{:S(2)}) async-start(f32[32,1,512]{2,1,0:T(1,128)} %copy.10), calls=%async_computation.7 | async-start | bytes 131072 | tf_op jit(solution)/shard_map/all_to_all | solution.py:27
  352.5 13.3 %all-to-all-start.9 = ((f32[32,1,512]{2,1,0:T(1,128)}), f32[32,1,512]{2,1,0:T(1,128)S(1)}, u32[]{:S(2)}, u32[]{:S(2)}) async-start(f32[32,1,512]{2,1,0:T(1,128)} %copy.11), calls=%async_computation.9 | async-start | bytes 131072 | tf_op jit(solution)/shard_map/all_to_all | solution.py:27
  366.4 12.7 %all-to-all-start.8 = ((f32[32,1,512]{2,1,0:T(1,128)}), f32[32,1,512]{2,1,0:T(1,128)S(1)}, u32[]{:S(2)}, u32[]{:S(2)}) async-start(f32[32,1,512]{2,1,0:T(1,128)} %broadcast_in_dim.12), calls=%async_computation.8 | async-start | bytes 131072 | tf_op jit(solution)/shard_map/all_to_all | solution.py:46
  379.9 13.5 %all-to-all-start.10 = ((f32[32,1,512]{2,1,0:T(1,128)}), f32[32,1,512]{2,1,0:T(1,128)}, u32[]{:S(2)}, u32[]{:S(2)}) async-start(f32[32,1,512]{2,1,0:T(1,128)} %broadcast_in_dim.13), calls=%async_computation.10 | async-start | bytes 131072 | tf_op jit(solution)/shard_map/all_to_all | solution.py:46
  393.4 30.7 %all-to-all-start.2 = ((f32[16,32,384]{2,1,0:T(8,128)}), f32[16,32,384]{2,1,0:T(8,128)}, u32[]{:S(2)}, u32[]{:S(2)}) async-start(f32[16,32,384]{2,1,0:T(8,128)} %bitcast.122), calls=%async_computation.2 | async-start | bytes 1572864 | tf_op jit(solution)/shard_map/all_to_all | solution.py:27
  400.8 55.6 %all-gather.8.cloned.1.call-start = ((), (), s32[]{:S(2)}) async-start(), calls=%async_computation.15 | async-start | bytes 1114112 | tf_op jit(solution)/shard_map/all_gather | solution.py:106
  404.6 42.9 %copy-start.4 = (f32[32,512]{1,0:T(8,128)S(1)}, f32[32,512]{1,0:T(8,128)}, u32[]{:S(2)}) copy-start(f32[32,512]{1,0:T(8,128)} %convolution_add_fusion.3) | copy-start | bytes 196612
  406.7 25.8 %copy-start.10 = (f32[384]{0:T(512)S(1)}, f32[384]{0:T(512)}, u32[]{:S(2)}) copy-start(f32[384]{0:T(512)} %convolution_reduce_fusion.3) | copy-start | bytes 4612
  427.3 30.9 %copy-start.6 = (f32[32,512]{1,0:T(8,128)S(1)}, f32[32,512]{1,0:T(8,128)}, u32[]{:S(2)}) copy-start(f32[32,512]{1,0:T(8,128)} %copy-done.5) | copy-start | bytes 196612
  428.0 13.4 %all-to-all-start.11 = ((f32[32,1,512]{2,1,0:T(1,128)}), f32[32,1,512]{2,1,0:T(1,128)}, u32[]{:S(2)}, u32[]{:S(2)}) async-start(f32[32,1,512]{2,1,0:T(1,128)} %copy.12), calls=%async_computation.11 | async-start | bytes 131072 | tf_op jit(solution)/shard_map/all_to_all | solution.py:27
  442.9 13.5 %all-to-all-start.12 = ((f32[32,1,512]{2,1,0:T(1,128)}), f32[32,1,512]{2,1,0:T(1,128)}, u32[]{:S(2)}, u32[]{:S(2)}) async-start(f32[32,1,512]{2,1,0:T(1,128)} %broadcast_in_dim.14), calls=%async_computation.12 | async-start | bytes 131072 | tf_op jit(solution)/shard_map/all_to_all | solution.py:46
  (6 other events, 15.1 us)
Sparse Core Ops, SparseCore 0:
  11.2 91.5 all-gather.3
  108.1 87.3 all-reduce.4
  198.6 41.2 all-reduce.6
  315.2 39.2 all-gather.5
  404.7 38.7 all-gather.7
where the time goes:
time: 467 us; the launch traced here: 465 us
  waiting for transfers between devices  310 us (66%)
  starting transfers between devices  74.1 us (16%)
  matrix products  40.5 us (9%)
  other arithmetic  17.4 us (4%)
  between operations  14.1 us (3%)
  local copies, waits for them, and re-layouts  9.62 us (2%)
    psum x2, waiting for transfers between devices, broadcast_by_axis(): x = lax.psum(x, axis)  95.9 us
    all_to_all x8, waiting for transfers between devices, sent_and_summed(): pieces = lax.all_to_all(split_up(x, dim, length), axis, 0, 0, tiled=True)  94.9 us
    all_gather x1, waiting for transfers between devices, body(): fetched = lax.all_gather(factor_front, 'col', axis=2, tiled=True)  91.5 us
    all_to_all x8, starting transfers between devices, sent_and_summed(): pieces = lax.all_to_all(split_up(x, dim, length), axis, 0, 0, tiled=True)  53 us
    all_to_all x5, waiting for transfers between devices, from_everyone(): return lax.all_to_all(copies, axis, split_axis=0, concat_axis=0, tiled=True)  26.6 us
    dot_general x7, matrix products, contract_first(): lax.dot_general(former, latter, (((0,), (0,)), ((), ())), precision=HIGH,...  22.4 us
    all_to_all x5, starting transfers between devices, from_everyone(): return lax.all_to_all(copies, axis, split_axis=0, concat_axis=0, tiled=True)  20.7 us
    dot_general x7, matrix products, matmul(): jnp.dot(former, latter, precision=HIGH, preferred_element_type=jnp.float32)  13.3 us
  transfers between devices with their start and end apart: 18, of which 16 were waited for; matrix products, arithmetic and copies ran while one was open for 12% of the time, Pallas kernels for 0%

commit v1 on v0

--- a/solution.py
+++ b/solution.py
@@ -7,6 +7,13 @@
 BLK = 128
 ROW = ("row_0", "row_1")
 HIGH = lax.Precision.HIGHEST
+
+
+def gather_over(shard, axis, dim):
+    peers = lax.axis_size(axis)
+    parts = jnp.stack([shard for _ in range(peers)])
+    parts = lax.all_to_all(parts, axis, split_axis=0, concat_axis=0)
+    return jnp.concatenate(parts, axis=dim)
 
 
 def broadcast_by_axis(x, axes, root):
@@ -84,7 +91,7 @@
     supers = structure.shape[0]
     row_first = row_index * rows_here
     col_first = col_index * cols_here
-    fetched = lax.all_gather(factor_front, "col", axis=2, tiled=True)
+    fetched = gather_over(factor_front, "col", 2)
     fronts = []
     parents = []
     diagonals = []

time: 467 us -> 498 us (1.066)
  waiting for transfers between devices: 310 us -> 325 us
  starting transfers between devices: 74.1 us -> 84.9 us
  local copies, waits for them, and re-layouts: 9.62 us -> 18.2 us
    all_to_all x0 -> x1, waiting for transfers between devices: none -> 103 us  [gather_over(): parts = lax.all_to_all(parts, axis, split_axis=0, concat_axis=0)]
    all_gather x1 -> x0, waiting for transfers between devices: 91.5 us -> none  [body(): fetched = lax.all_gather(factor_front, 'col', axis=2, tiled=True)]
    all_to_all x0 -> x1, starting transfers between devices: none -> 10.7 us  [gather_over(): parts = lax.all_to_all(parts, axis, split_axis=0, concat_axis=0)]
  transfers between devices with their start and end apart: 18 -> 18, of which waited for: 16 -> 16; matrix products, arithmetic and copies ran while one was open for 12% -> 11% of each run, Pallas kernels for 0% -> 0%
where the time goes in v1:
time: 498 us; the launch traced here: 496 us
  waiting for transfers between devices  325 us (65%)
  starting transfers between devices  84.9 us (17%)
  matrix products  38.5 us (8%)
  local copies, waits for them, and re-layouts  18.2 us (4%)
  other arithmetic  15.4 us (3%)
  between operations  14.2 us (3%)
    all_to_all x1, waiting for transfers between devices, gather_over(): parts = lax.all_to_all(parts, axis, split_axis=0, concat_axis=0)  103 us
    psum x2, waiting for transfers between devices, broadcast_by_axis(): x = lax.psum(x, axis)  101 us
    all_to_all x8, waiting for transfers between devices, sent_and_summed(): pieces = lax.all_to_all(split_up(x, dim, length), axis, 0, 0, tiled=True)  94.8 us
    all_to_all x8, starting transfers between devices, sent_and_summed(): pieces = lax.all_to_all(split_up(x, dim, length), axis, 0, 0, tiled=True)  52.9 us
    all_to_all x5, waiting for transfers between devices, from_everyone(): return lax.all_to_all(copies, axis, split_axis=0, concat_axis=0, tiled=True)  26.3 us
    dot_general x7, matrix products, contract_first(): lax.dot_general(former, latter, (((0,), (0,)), ((), ())), precision=HIGH,...  22.4 us
    all_to_all x5, starting transfers between devices, from_everyone(): return lax.all_to_all(copies, axis, split_axis=0, concat_axis=0, tiled=True)  20.9 us
    dot_general x7, matrix products, matmul(): jnp.dot(former, latter, precision=HIGH, preferred_element_type=jnp.float32)  13.3 us
  transfers between devices with their start and end apart: 18, of which 16 were waited for; matrix products, arithmetic and copies ran while one was open for 11% of the time, Pallas kernels for 0%

profile of v1, /device:TPU:1, one launch (start us, length us, event | category | flops | bytes accessed | tf_op | source)
XLA Modules:
  0.0 496.3 jit_solution(9563995603728379249)
XLA Ops:
  11.0 10.7 %all-to-all-start = ((f32[32,3,768,16]{2,3,1,0:T(8,128)}), f32[32,3,768,16]{2,3,1,0:T(8,128)}, u32[]{:S(2)}, u32[]{:S(2)}) async-start(f32[32,3,768,16]{2,3,1,0:T(8,128)} %stack.16), calls=%async_computation | async-start | bytes 9437184 | tf_op jit(solution)/shard_map/all_to_all | solution.py:15
  23.0 103.3 %all-to-all-done = f32[32,3,768,16]{2,3,1,0:T(8,128)} async-done(((f32[32,3,768,16]{2,3,1,0:T(8,128)}), f32[32,3,768,16]{2,3,1,0:T(8,128)}, u32[]{:S(2)}, u32[]{:S(2)}) %all-to-all-start) | async-done | bytes 4718624 | tf_op jit(solution)/shard_map/all_to_all | solution.py:15
  134.4 92.2 %all-reduce.5.cloned.1.call-done = (f32[384,512]{0,1:T(8,128)}, f32[384,512]{0,1:T(8,128)}, f32[384,512]{0,1:T(8,128)}) async-done(((f32[384,512]{0,1:T(8,128)}, f32[384,512]{0,1:T(8,128)}, f32[384,512]{0,1:T(8,128)}), (f32[384,512]{0,1:T(8,128)}, f32[384,512]{0,1:T(8,128)}, f32[384,512]{0,1:T(8,128)})) %all-reduce.5.cloned.1.call-update) | async-done | bytes 2359312 | tf_op jit(solution)/shard_map/psum | solution.py:22
  230.3 8.2 %all-to-all-start.1 = ((f32[16,32,384]{2,1,0:T(8,128)}), f32[16,32,384]{2,1,0:T(8,128)}, u32[]{:S(2)}, u32[]{:S(2)}) async-start(f32[16,32,384]{2,1,0:T(8,128)} %fusion), calls=%async_computation.1 | async-start | bytes 1572864 | tf_op jit(solution)/shard_map/all_to_all | solution.py:34
  238.8 22.4 %all-to-all-done.1 = f32[16,32,384]{2,1,0:T(8,128)} async-done(((f32[16,32,384]{2,1,0:T(8,128)}), f32[16,32,384]{2,1,0:T(8,128)}, u32[]{:S(2)}, u32[]{:S(2)}) %all-to-all-start.1) | async-done | bytes 786464 | tf_op jit(solution)/shard_map/all_to_all | solution.py:34
  262.4 8.5 %all-reduce.7.cloned.1.call-done = (f32[384,512]{0,1:T(8,128)}, f32[384,512]{0,1:T(8,128)}, f32[384,512]{0,1:T(8,128)}) async-done(((f32[384,512]{0,1:T(8,128)}, f32[384,512]{0,1:T(8,128)}, f32[384,512]{0,1:T(8,128)}), (f32[384,512]{0,1:T(8,128)}, f32[384,512]{0,1:T(8,128)}, f32[384,512]{0,1:T(8,128)})) %all-reduce.7.cloned.1.call-update) | async-done | bytes 2359312 | tf_op jit(solution)/shard_map/psum | solution.py:22
  273.6 8.3 %all-to-all-start.6 = ((f32[32,1,512]{2,1,0:T(1,128)}), f32[32,1,512]{2,1,0:T(1,128)S(1)}, u32[]{:S(2)}, u32[]{:S(2)}) async-start(f32[32,1,512]{2,1,0:T(1,128)} %copy.9), calls=%async_computation.6 | async-start | bytes 131072 | tf_op jit(solution)/shard_map/all_to_all | solution.py:34
  284.6 6.2 %all-to-all-done.6 = f32[32,1,512]{2,1,0:T(1,128)S(1)} async-done(((f32[32,1,512]{2,1,0:T(1,128)}), f32[32,1,512]{2,1,0:T(1,128)S(1)}, u32[]{:S(2)}, u32[]{:S(2)}) %all-to-all-start.6) | async-done | bytes 65568 | tf_op jit(solution)/shard_map/all_to_all | solution.py:34
  296.2 7.2 %all-to-all-done.4 = f32[32,1,512]{2,1,0:T(1,128)S(1)} async-done(((f32[32,1,512]{2,1,0:T(1,128)}), f32[32,1,512]{2,1,0:T(1,128)S(1)}, u32[]{:S(2)}, u32[]{:S(2)}) %all-to-all-start.4) | async-done | bytes 65568 | tf_op jit(solution)/shard_map/all_to_all | solution.py:34
  310.6 6.2 %all-to-all-done.7 = f32[32,1,512]{2,1,0:T(1,128)S(1)} async-done(((f32[32,1,512]{2,1,0:T(1,128)}), f32[32,1,512]{2,1,0:T(1,128)S(1)}, u32[]{:S(2)}, u32[]{:S(2)}) %all-to-all-start.7) | async-done | bytes 65568 | tf_op jit(solution)/shard_map/all_to_all | solution.py:53
  321.6 5.1 %convolution_add_fusion.1 = f32[512,384]{1,0:T(8,128)} fusion(f32[512,384]{1,0:T(8,128)} %fusion.18, f32[768,512]{0,1:T(8,128)} %copy-done.3, f32[768,384]{1,0:T(8,128)S(1)} %copy-done), kind=kOutput, calls=%fused_computation.4 | convolution fusion | flops 1812135936 | bytes 4325376 | tf_op jit(solution)/shard_map/dot_general | solution.py:72
  330.2 12.6 %all-to-all-start.2 = ((f32[16,32,384]{2,1,0:T(8,128)}), f32[16,32,384]{2,1,0:T(8,128)}, u32[]{:S(2)}, u32[]{:S(2)}) async-start(f32[16,32,384]{2,1,0:T(8,128)} %bitcast.118), calls=%async_computation.2 | async-start | bytes 1572864 | tf_op jit(solution)/shard_map/all_to_all | solution.py:34
  346.3 19.9 %all-to-all-done.2 = f32[16,32,384]{2,1,0:T(8,128)} async-done(((f32[16,32,384]{2,1,0:T(8,128)}), f32[16,32,384]{2,1,0:T(8,128)}, u32[]{:S(2)}, u32[]{:S(2)}) %all-to-all-start.2) | async-done | bytes 786464 | tf_op jit(solution)/shard_map/all_to_all | solution.py:34
  376.8 6.2 %all-to-all-done.8 = f32[32,1,512]{2,1,0:T(1,128)S(1)} async-done(((f32[32,1,512]{2,1,0:T(1,128)}), f32[32,1,512]{2,1,0:T(1,128)S(1)}, u32[]{:S(2)}, u32[]{:S(2)}) %all-to-all-start.8) | async-done | bytes 65568 | tf_op jit(solution)/shard_map/all_to_all | solution.py:34
  388.4 8.5 %all-to-all-done.10 = f32[32,1,512]{2,1,0:T(1,128)S(1)} async-done(((f32[32,1,512]{2,1,0:T(1,128)}), f32[32,1,512]{2,1,0:T(1,128)S(1)}, u32[]{:S(2)}, u32[]{:S(2)}) %all-to-all-start.10) | async-done | bytes 65568 | tf_op jit(solution)/shard_map/all_to_all | solution.py:34
  404.9 5.4 %all-to-all-done.9 = f32[32,1,512]{2,1,0:T(1,128)S(1)} async-done(((f32[32,1,512]{2,1,0:T(1,128)}), f32[32,1,512]{2,1,0:T(1,128)S(1)}, u32[]{:S(2)}, u32[]{:S(2)}) %all-to-all-start.9) | async-done | bytes 65568 | tf_op jit(solution)/shard_map/all_to_all | solution.py:53
  411.0 4.6 all-to-all-start.11
  415.5 5.1 %convolution_add_fusion = f32[512,384]{1,0:T(8,128)} fusion(f32[512,384]{1,0:T(8,128)} %fusion.16, f32[768,512]{0,1:T(8,128)} %copy-done.2, f32[768,384]{1,0:T(8,128)S(1)} %copy-done), kind=kOutput, calls=%fused_computation.3 | convolution fusion | flops 1812135936 | bytes 4325376 | tf_op jit(solution)/shard_map/dot_general | solution.py:72
  424.5 7.5 %all-to-all-start.3 = ((f32[16,32,384]{2,1,0:T(8,128)}), f32[16,32,384]{2,1,0:T(8,128)}, u32[]{:S(2)}, u32[]{:S(2)}) async-start(f32[16,32,384]{2,1,0:T(8,128)} %bitcast.117), calls=%async_computation.3 | async-start | bytes 1572864 | tf_op jit(solution)/shard_map/all_to_all | solution.py:34
  438.1 17.0 %all-to-all-done.3 = f32[16,32,384]{2,1,0:T(8,128)} async-done(((f32[16,32,384]{2,1,0:T(8,128)}), f32[16,32,384]{2,1,0:T(8,128)}, u32[]{:S(2)}, u32[]{:S(2)}) %all-to-all-start.3) | async-done | bytes 786464 | tf_op jit(solution)/shard_map/all_to_all | solution.py:34
  459.0 4.6 all-to-all-start.12
  465.0 7.3 %all-to-all-done.12 = f32[32,1,512]{2,1,0:T(1,128)} async-done(((f32[32,1,512]{2,1,0:T(1,128)}), f32[32,1,512]{2,1,0:T(1,128)}, u32[]{:S(2)}, u32[]{:S(2)}) %all-to-all-start.12) | async-done | bytes 65568 | tf_op jit(solution)/shard_map/all_to_all | solution.py:34
  473.9 4.6 all-to-all-start.13
  480.0 7.3 %all-to-all-done.13 = f32[32,1,512]{2,1,0:T(1,128)} async-done(((f32[32,1,512]{2,1,0:T(1,128)}), f32[32,1,512]{2,1,0:T(1,128)}, u32[]{:S(2)}, u32[]{:S(2)}) %all-to-all-start.13) | async-done | bytes 65568 | tf_op jit(solution)/shard_map/all_to_all | solution.py:53
  (98 shorter events, 93.2 us)
Async XLA Ops:
  7.2 219.5 %copy-start = (f32[768,384]{1,0:T(8,128)S(1)}, f32[768,384]{1,0:T(8,128)}, u32[]{:S(2)}) copy-start(f32[768,384]{1,0:T(8,128)} %param.5) | copy-start | bytes 3538948
  11.0 115.3 %all-to-all-start = ((f32[32,3,768,16]{2,3,1,0:T(8,128)}), f32[32,3,768,16]{2,3,1,0:T(8,128)}, u32[]{:S(2)}, u32[]{:S(2)}) async-start(f32[32,3,768,16]{2,3,1,0:T(8,128)} %stack.16), calls=%async_computation | async-start | bytes 9437184 | tf_op jit(solution)/shard_map/all_to_all | solution.py:15
  21.7 204.9 %all-reduce.5.cloned.1.call-start = ((), (), s32[]{:S(2)}) async-start(), calls=%async_computation.16 | async-start | bytes 4718592 | tf_op jit(solution)/shard_map/psum | solution.py:22
  134.4 136.6 %all-reduce.7.cloned.1.call-start = ((), (), s32[]{:S(2)}) async-start(), calls=%async_computation.17 | async-start | bytes 4718592 | tf_op jit(solution)/shard_map/psum | solution.py:22
  230.3 31.0 %all-to-all-start.1 = ((f32[16,32,384]{2,1,0:T(8,128)}), f32[16,32,384]{2,1,0:T(8,128)}, u32[]{:S(2)}, u32[]{:S(2)}) async-start(f32[16,32,384]{2,1,0:T(8,128)} %fusion), calls=%async_computation.1 | async-start | bytes 1572864 | tf_op jit(solution)/shard_map/all_to_all | solution.py:34
  238.8 55.8 %copy-start.1 = (f32[2,512,512]{2,1,0:T(8,128)S(1)}, f32[2,512,512]{2,1,0:T(8,128)}, u32[]{:S(2)}) copy-start(f32[2,512,512]{2,1,0:T(8,128)} %param.8) | copy-start | bytes 6291460
  273.6 17.1 %all-to-all-start.6 = ((f32[32,1,512]{2,1,0:T(1,128)}), f32[32,1,512]{2,1,0:T(1,128)S(1)}, u32[]{:S(2)}, u32[]{:S(2)}) async-start(f32[32,1,512]{2,1,0:T(1,128)} %copy.9), calls=%async_computation.6 | async-start | bytes 131072 | tf_op jit(solution)/shard_map/all_to_all | solution.py:34
  290.7 12.7 %all-to-all-start.4 = ((f32[32,1,512]{2,1,0:T(1,128)}), f32[32,1,512]{2,1,0:T(1,128)S(1)}, u32[]{:S(2)}, u32[]{:S(2)}) async-start(f32[32,1,512]{2,1,0:T(1,128)} %copy.8), calls=%async_computation.4 | async-start | bytes 131072 | tf_op jit(solution)/shard_map/all_to_all | solution.py:34
  304.1 12.7 %all-to-all-start.7 = ((f32[32,1,512]{2,1,0:T(1,128)}), f32[32,1,512]{2,1,0:T(1,128)S(1)}, u32[]{:S(2)}, u32[]{:S(2)}) async-start(f32[32,1,512]{2,1,0:T(1,128)} %broadcast_in_dim.11), calls=%async_computation.7 | async-start | bytes 131072 | tf_op jit(solution)/shard_map/all_to_all | solution.py:53
  317.5 12.7 %all-to-all-start.5 = ((f32[32,1,512]{2,1,0:T(1,128)}), f32[32,1,512]{2,1,0:T(1,128)S(1)}, u32[]{:S(2)}, u32[]{:S(2)}) async-start(f32[32,1,512]{2,1,0:T(1,128)} %broadcast_in_dim.10), calls=%async_computation.5 | async-start | bytes 131072 | tf_op jit(solution)/shard_map/all_to_all | solution.py:53
  330.2 12.6 %copy-start.7 = (f32[32,1,512]{2,1,0:T(1,128)}, f32[32,1,512]{2,1,0:T(1,128)S(1)}, u32[]{:S(2)}) copy-start(f32[32,1,512]{2,1,0:T(1,128)S(1)} %all-to-all-done.5) | copy-start | bytes 196612
  330.2 35.9 %all-to-all-start.2 = ((f32[16,32,384]{2,1,0:T(8,128)}), f32[16,32,384]{2,1,0:T(8,128)}, u32[]{:S(2)}, u32[]{:S(2)}) async-start(f32[16,32,384]{2,1,0:T(8,128)} %bitcast.118), calls=%async_computation.2 | async-start | bytes 1572864 | tf_op jit(solution)/shard_map/all_to_all | solution.py:34
  342.9 89.4 %all-gather.3.cloned.1.call-start = ((), (), s32[]{:S(2)}) async-start(), calls=%async_computation.14 | async-start | bytes 1114112 | tf_op jit(solution)/shard_map/all_gather | solution.py:113
  370.0 13.0 %all-to-all-start.8 = ((f32[32,1,512]{2,1,0:T(1,128)}), f32[32,1,512]{2,1,0:T(1,128)S(1)}, u32[]{:S(2)}, u32[]{:S(2)}) async-start(f32[32,1,512]{2,1,0:T(1,128)} %copy.10), calls=%async_computation.8 | async-start | bytes 131072 | tf_op jit(solution)/shard_map/all_to_all | solution.py:34
  383.6 13.3 %all-to-all-start.10 = ((f32[32,1,512]{2,1,0:T(1,128)}), f32[32,1,512]{2,1,0:T(1,128)S(1)}, u32[]{:S(2)}, u32[]{:S(2)}) async-start(f32[32,1,512]{2,1,0:T(1,128)} %copy.11), calls=%async_computation.10 | async-start | bytes 131072 | tf_op jit(solution)/shard_map/all_to_all | solution.py:34
  397.6 12.7 %all-to-all-start.9 = ((f32[32,1,512]{2,1,0:T(1,128)}), f32[32,1,512]{2,1,0:T(1,128)S(1)}, u32[]{:S(2)}, u32[]{:S(2)}) async-start(f32[32,1,512]{2,1,0:T(1,128)} %broadcast_in_dim.12), calls=%async_computation.9 | async-start | bytes 131072 | tf_op jit(solution)/shard_map/all_to_all | solution.py:53
  411.0 13.5 %all-to-all-start.11 = ((f32[32,1,512]{2,1,0:T(1,128)}), f32[32,1,512]{2,1,0:T(1,128)}, u32[]{:S(2)}, u32[]{:S(2)}) async-start(f32[32,1,512]{2,1,0:T(1,128)} %broadcast_in_dim.13), calls=%async_computation.11 | async-start | bytes 131072 | tf_op jit(solution)/shard_map/all_to_all | solution.py:53
  424.5 30.6 %all-to-all-start.3 = ((f32[16,32,384]{2,1,0:T(8,128)}), f32[16,32,384]{2,1,0:T(8,128)}, u32[]{:S(2)}, u32[]{:S(2)}) async-start(f32[16,32,384]{2,1,0:T(8,128)} %bitcast.117), calls=%async_computation.3 | async-start | bytes 1572864 | tf_op jit(solution)/shard_map/all_to_all | solution.py:34
  431.9 55.4 %all-gather.5.cloned.1.call-start = ((), (), s32[]{:S(2)}) async-start(), calls=%async_computation.15 | async-start | bytes 1114112 | tf_op jit(solution)/shard_map/all_gather | solution.py:113
  435.9 42.6 %copy-start.4 = (f32[32,512]{1,0:T(8,128)S(1)}, f32[32,512]{1,0:T(8,128)}, u32[]{:S(2)}) copy-start(f32[32,512]{1,0:T(8,128)} %convolution_add_fusion.3) | copy-start | bytes 196612
  438.1 25.4 %copy-start.10 = (f32[384]{0:T(512)S(1)}, f32[384]{0:T(512)}, u32[]{:S(2)}) copy-start(f32[384]{0:T(512)} %convolution_reduce_fusion.3) | copy-start | bytes 4612
  458.2 30.8 %copy-start.6 = (f32[32,512]{1,0:T(8,128)S(1)}, f32[32,512]{1,0:T(8,128)}, u32[]{:S(2)}) copy-start(f32[32,512]{1,0:T(8,128)} %copy-done.5) | copy-start | bytes 196612
  459.0 13.4 %all-to-all-start.12 = ((f32[32,1,512]{2,1,0:T(1,128)}), f32[32,1,512]{2,1,0:T(1,128)}, u32[]{:S(2)}, u32[]{:S(2)}) async-start(f32[32,1,512]{2,1,0:T(1,128)} %copy.12), calls=%async_computation.12 | async-start | bytes 131072 | tf_op jit(solution)/shard_map/all_to_all | solution.py:34
  473.9 13.4 %all-to-all-start.13 = ((f32[32,1,512]{2,1,0:T(1,128)}), f32[32,1,512]{2,1,0:T(1,128)}, u32[]{:S(2)}, u32[]{:S(2)}) async-start(f32[32,1,512]{2,1,0:T(1,128)} %broadcast_in_dim.14), calls=%async_computation.13 | async-start | bytes 131072 | tf_op jit(solution)/shard_map/all_to_all | solution.py:53
  (6 other events, 15.1 us)
Sparse Core Ops, SparseCore 0:
  134.5 92.1 all-reduce.4
  229.7 41.2 all-reduce.6
  346.6 38.9 all-gather.2
  436.1 38.5 all-gather.4
